TPU v7x, 128 devices: a whole 4x4x4 slice. The times are simulated.
128 devices in a mesh: ctx: 8 (over y, x_hi), fsdp: 16 (over z, x_lo, core).
Axes of the slice: x: 4 (x_hi: 2, x_lo: 2; x = x_hi * 2 + x_lo), y: 4, z: 4, core: 2. Of those that a mesh axis runs over, the one named last changes fastest.
Arguments:
- tokens: bfloat16 [16384, 640], P(('ctx', 'fsdp')), may hold values from -6 to 6
- query_weight: bfloat16 [640, 1024], P(('ctx', 'fsdp')), may hold values from -0.25 to 0.25
- key_weight: bfloat16 [640, 256], P(('ctx', 'fsdp')), may hold values from -0.25 to 0.25
- value_weight: bfloat16 [640, 256], P(('ctx', 'fsdp')), may hold values from -0.25 to 0.25
- output_weight: bfloat16 [1024, 640], P(('ctx', 'fsdp')), may hold values from -0.1875 to 0.1875
- gate_weight: bfloat16 [640, 2048], P('ctx', 'fsdp'), may hold values from -0.25 to 0.25
- up_weight: bfloat16 [640, 2048], P('ctx', 'fsdp'), may hold values from -0.25 to 0.25
- down_weight: bfloat16 [2048, 640], P('fsdp', 'ctx'), may hold values from -0.125 to 0.125
- input_gain: bfloat16 [640], P(('ctx', 'fsdp')), may hold values from -0.5 to 0.5
- attention_gain: bfloat16 [640], P(('ctx', 'fsdp')), may hold values from -0.5 to 0.5
- feedforward_gain: bfloat16 [640], P(('ctx', 'fsdp')), may hold values from -0.5 to 0.5
- output_gain: bfloat16 [640], P(('ctx', 'fsdp')), may hold values from -0.5 to 0.5
- block_table: int32 [16], replicated, may hold values from 0 to 15, as said below
- cotangent: bfloat16 [16384, 640], P(('ctx', 'fsdp')), may hold values from -6 to 6
Outputs:
- output: bfloat16 [16384, 640], P(('ctx', 'fsdp'))
- tokens_gradient: bfloat16 [16384, 640], P(('ctx', 'fsdp'))
- query_gradient: float32 [640, 1024], P(('ctx', 'fsdp'))
- key_gradient: float32 [640, 256], P(('ctx', 'fsdp'))
- value_gradient: float32 [640, 256], P(('ctx', 'fsdp'))
- projection_gradient: float32 [1024, 640], P(('ctx', 'fsdp'))
- gate_gradient: float32 [640, 2048], P('ctx', 'fsdp')
- up_gradient: float32 [640, 2048], P('ctx', 'fsdp')
- down_gradient: float32 [2048, 640], P('fsdp', 'ctx')
- input_gain_gradient: float32 [640], P(('ctx', 'fsdp'))
- attention_gain_gradient: float32 [640], P(('ctx', 'fsdp'))
- feedforward_gain_gradient: float32 [640], P(('ctx', 'fsdp'))
- output_gain_gradient: float32 [640], P(('ctx', 'fsdp'))
Inputs may be any that keep to these rules, and one draw needn't show every extreme that they name: `block_table`: the two slots of each index of ctx hold blocks p and 15 - p for some p, in either order; every block stands in exactly one slot.
All inputs are finite; a program needn't handle non-finite values.
Results may differ from a plain program's by a relative error of at most 0.04.
Values may be sent and summed in bfloat16 or wider, within the bound.
A program may use at most 128 MiB of HBM per device.

v0:
```python
from functools import partial

import jax
import jax.numpy as jnp
from jax import lax
from jax.sharding import PartitionSpec as P

H = 4
KVH = 1
HD = 256


softcap = 50.0
epsilon = 1e-06
masked_value = -1e30


def rms_scale(value):
    return lax.rsqrt(jnp.mean(value * value, axis=-1, keepdims=True) + epsilon)


def norm_forward(value, gain):
    return value * rms_scale(value) * (1.0 + gain)


def norm_backward(value, gain, upstream):
    scale = rms_scale(value)
    normed = value * scale
    gain_part = jnp.sum(upstream * normed, axis=0)
    inner = upstream * (1.0 + gain)
    result = scale * (inner - normed * jnp.mean(inner * normed, axis=-1, keepdims=True))
    return (result, gain_part)


def product(left, right):
    return jnp.dot(left, right, preferred_element_type=jnp.float32)


def inner_rows(left, right):
    return lax.dot_general(
        left, right, (((0,), (0,)), ((), ())), preferred_element_type=jnp.float32
    )


def outer_cols(left, right):
    return lax.dot_general(
        left, right, (((1,), (1,)), ((), ())), preferred_element_type=jnp.float32
    )


def gated(gate, up):
    return jax.nn.gelu(gate, approximate=True) * up


def table_lookup(table, slots):
    hits = slots[:, None] == jnp.arange(table.shape[0], dtype=jnp.int32)[None, :]
    return jnp.sum(jnp.where(hits, table[None, :], 0), axis=1)


def split_query(array):
    return jnp.moveaxis(array.reshape(array.shape[0], H, HD), 1, 0)


def split_shared(array):
    heads = jnp.moveaxis(array.reshape(array.shape[0], KVH, HD), 1, 0)
    return jnp.repeat(heads, H // KVH, axis=0)


def join_query(array):
    return jnp.moveaxis(array, 0, 1).reshape(array.shape[1], H * HD)


def fold_shared(array):
    summed = jnp.sum(array.reshape(KVH, H // KVH, array.shape[1], HD), axis=1)
    return jnp.moveaxis(summed, 0, 1).reshape(array.shape[1], KVH * HD)


def fetch_attention(
    query_weight,
    key_weight,
    value_weight,
    output_weight,
    input_gain,
    attention_gain,
    feedforward_gain,
    output_gain,
):
    return (
        lax.all_gather(query_weight, ("ctx", "fsdp"), axis=0, tiled=True),
        lax.all_gather(key_weight, ("ctx", "fsdp"), axis=0, tiled=True),
        lax.all_gather(value_weight, ("ctx", "fsdp"), axis=0, tiled=True),
        lax.all_gather(output_weight, ("ctx", "fsdp"), axis=0, tiled=True),
        lax.all_gather(input_gain, ("ctx", "fsdp"), axis=0, tiled=True),
        lax.all_gather(attention_gain, ("ctx", "fsdp"), axis=0, tiled=True),
        lax.all_gather(feedforward_gain, ("ctx", "fsdp"), axis=0, tiled=True),
        lax.all_gather(output_gain, ("ctx", "fsdp"), axis=0, tiled=True),
    )


def fetch_feedforward(gate_weight, up_weight, down_weight):
    return (
        lax.all_gather(gate_weight, "ctx", axis=0, tiled=True),
        lax.all_gather(up_weight, "ctx", axis=0, tiled=True),
        lax.all_gather(down_weight, "ctx", axis=1, tiled=True),
    )


def scores_of(query_head, key_head):
    return outer_cols(query_head, key_head) * HD ** (-0.5)


def partial_forward(allowed, items):
    query_head, key_head, value_head = items
    capped = softcap * jnp.tanh(scores_of(query_head, key_head) / softcap)
    capped = jnp.where(allowed, capped, masked_value)
    peak = jnp.max(capped, axis=-1)
    weights = jnp.exp(capped - peak[:, None])
    total = jnp.sum(weights, axis=-1)
    summed = product(weights.astype(jnp.bfloat16), value_head)
    return (summed, peak, total)


def partial_backward(allowed, items):
    query_head, key_head, value_head, grad_head, delta_head, lse_head = items
    tangent = jnp.tanh(scores_of(query_head, key_head) / softcap)
    probs = jnp.where(allowed, jnp.exp(softcap * tangent - lse_head[:, None]), 0.0)
    value_grad = inner_rows(probs.astype(jnp.bfloat16), grad_head)
    prob_grad = outer_cols(grad_head, value_head)
    score_grad = (probs * (prob_grad - delta_head[:, None]) * (1.0 - tangent * tangent)).astype(
        jnp.bfloat16
    )
    query_grad = product(score_grad, key_head) * HD ** (-0.5)
    key_grad = inner_rows(score_grad, query_head) * HD ** (-0.5)
    return (query_grad, key_grad, value_grad)


def shards(
    tokens,
    query_weight,
    key_weight,
    value_weight,
    output_weight,
    gate_weight,
    up_weight,
    down_weight,
    input_gain,
    attention_gain,
    feedforward_gain,
    output_gain,
    block_table,
    cotangent,
):
    ctx_size = lax.axis_size("ctx")
    fsdp_size = lax.axis_size("fsdp")
    own_rows = tokens.shape[0]
    group_rows = own_rows * fsdp_size
    block_rows = group_rows // 2
    ctx_index = lax.axis_index("ctx")
    fsdp_index = lax.axis_index("fsdp")
    query_index = jnp.arange(group_rows, dtype=jnp.int32)
    query_pos = (
        table_lookup(block_table, 2 * ctx_index + query_index // block_rows) * block_rows
        + query_index % block_rows
    )
    key_index = jnp.arange(ctx_size * own_rows, dtype=jnp.int32)
    offset = fsdp_index * own_rows
    key_pos = (
        table_lookup(block_table, 2 * (key_index // own_rows) + offset // block_rows) * block_rows
        + offset % block_rows
        + key_index % own_rows
    )
    allowed = key_pos[None, :] <= query_pos[:, None]
    attention_full = fetch_attention(
        query_weight,
        key_weight,
        value_weight,
        output_weight,
        input_gain,
        attention_gain,
        feedforward_gain,
        output_gain,
    )
    query_full, key_full, value_full, output_full = (
        attention_full[0],
        attention_full[1],
        attention_full[2],
        attention_full[3],
    )
    input_scale = attention_full[4].astype(jnp.float32)
    attention_scale = attention_full[5].astype(jnp.float32)
    feedforward_scale = attention_full[6].astype(jnp.float32)
    output_scale = attention_full[7].astype(jnp.float32)
    gate_full, up_full, down_full = fetch_feedforward(gate_weight, up_weight, down_weight)
    tokens_float = tokens.astype(jnp.float32)
    normed_in = norm_forward(tokens_float, input_scale).astype(jnp.bfloat16)
    queries = product(normed_in, query_full).astype(jnp.bfloat16)
    keys = product(normed_in, key_full).astype(jnp.bfloat16)
    values = product(normed_in, value_full).astype(jnp.bfloat16)
    queries_all = lax.all_gather(queries, "fsdp", axis=0, tiled=True)
    keys_all, values_all = (
        lax.all_gather(keys, "ctx", axis=0, tiled=True),
        lax.all_gather(values, "ctx", axis=0, tiled=True),
    )
    query_heads = split_query(queries_all)
    key_heads = split_shared(keys_all)
    value_heads = split_shared(values_all)
    summed, peaks, totals = lax.map(
        partial(partial_forward, allowed), (query_heads, key_heads, value_heads)
    )
    part_sums, part_peaks, part_totals = (
        lax.all_to_all(
            join_query(summed).reshape(fsdp_size, own_rows, H * HD),
            "fsdp",
            split_axis=0,
            concat_axis=0,
            tiled=True,
        ),
        lax.all_to_all(
            jnp.transpose(peaks).reshape(fsdp_size, own_rows, H),
            "fsdp",
            split_axis=0,
            concat_axis=0,
            tiled=True,
        ),
        lax.all_to_all(
            jnp.transpose(totals).reshape(fsdp_size, own_rows, H),
            "fsdp",
            split_axis=0,
            concat_axis=0,
            tiled=True,
        ),
    )
    top = jnp.max(part_peaks, axis=0)
    factor = jnp.exp(part_peaks - top)
    denom = jnp.sum(part_totals * factor, axis=0)
    numer = jnp.sum(part_sums.reshape(fsdp_size, own_rows, H, HD) * factor[..., None], axis=0)
    attended = (numer / denom[..., None]).reshape(own_rows, H * HD)
    log_total = top + jnp.log(denom)
    attended_low = attended.astype(jnp.bfloat16)
    attention_out = product(attended_low, output_full)
    mixed = tokens_float + norm_forward(attention_out, attention_scale)
    normed_ffn = norm_forward(mixed, feedforward_scale).astype(jnp.bfloat16)
    normed_all = lax.all_gather(normed_ffn, "fsdp", axis=0, tiled=True)
    gate = product(normed_all, gate_full)
    up = product(normed_all, up_full)
    hidden, gated_pull = jax.vjp(gated, gate, up)
    hidden_low = hidden.astype(jnp.bfloat16)
    ffn_out = lax.psum_scatter(
        product(hidden_low, down_full), "fsdp", scatter_dimension=0, tiled=True
    )
    output = (mixed + norm_forward(ffn_out, output_scale)).astype(jnp.bfloat16)
    cotangent_float = cotangent.astype(jnp.float32)
    ffn_out_grad, output_gain_part = norm_backward(ffn_out, output_scale, cotangent_float)
    ffn_grad_low = ffn_out_grad.astype(jnp.bfloat16)
    held = lax.optimization_barrier((gate_weight, up_weight, down_weight, ffn_grad_low))
    ffn_grad_low = held[3]
    gate_back, up_back, down_back = fetch_feedforward(held[0], held[1], held[2])
    ffn_grad_all = lax.all_gather(ffn_grad_low, "fsdp", axis=0, tiled=True)
    down_part = inner_rows(hidden_low, ffn_grad_all)
    hidden_grad = outer_cols(ffn_grad_all, down_back)
    gate_grad, up_grad = gated_pull(hidden_grad)
    gate_low = gate_grad.astype(jnp.bfloat16)
    up_low = up_grad.astype(jnp.bfloat16)
    gate_part = inner_rows(normed_all, gate_low)
    up_part = inner_rows(normed_all, up_low)
    normed_ffn_grad = lax.psum_scatter(
        outer_cols(gate_low, gate_back) + outer_cols(up_low, up_back),
        "fsdp",
        scatter_dimension=0,
        tiled=True,
    )
    mixed_part, feedforward_gain_part = norm_backward(mixed, feedforward_scale, normed_ffn_grad)
    mixed_grad = cotangent_float + mixed_part
    attention_out_grad, attention_gain_part = norm_backward(
        attention_out, attention_scale, mixed_grad
    )
    out_grad_low = attention_out_grad.astype(jnp.bfloat16)
    held = lax.optimization_barrier(
        (
            query_weight,
            key_weight,
            value_weight,
            output_weight,
            input_gain,
            attention_gain,
            feedforward_gain,
            output_gain,
            out_grad_low,
        )
    )
    out_grad_low = held[8]
    fetched = fetch_attention(
        held[0], held[1], held[2], held[3], held[4], held[5], held[6], held[7]
    )
    query_back, key_back, value_back, output_back = (fetched[0], fetched[1], fetched[2], fetched[3])
    output_part = inner_rows(attended_low, out_grad_low)
    attended_grad = outer_cols(out_grad_low, output_back).astype(jnp.bfloat16)
    grad_float = attended_grad.astype(jnp.float32)
    delta = jnp.sum((grad_float * attended).reshape(own_rows, H, HD), axis=-1)
    grad_all, delta_all, lse_all = (
        lax.all_gather(grad_float, "fsdp", axis=0, tiled=True),
        lax.all_gather(delta, "fsdp", axis=0, tiled=True),
        lax.all_gather(log_total, "fsdp", axis=0, tiled=True),
    )
    query_parts, key_parts, value_parts = lax.map(
        partial(partial_backward, allowed),
        (
            query_heads,
            key_heads,
            value_heads,
            split_query(grad_all.astype(jnp.bfloat16)),
            jnp.transpose(delta_all),
            jnp.transpose(lse_all),
        ),
    )
    query_grad = lax.psum_scatter(
        join_query(query_parts), "fsdp", scatter_dimension=0, tiled=True
    ).astype(jnp.bfloat16)
    key_sum, value_sum = (
        lax.psum_scatter(fold_shared(key_parts), "ctx", scatter_dimension=0, tiled=True),
        lax.psum_scatter(fold_shared(value_parts), "ctx", scatter_dimension=0, tiled=True),
    )
    key_grad = key_sum.astype(jnp.bfloat16)
    value_grad = value_sum.astype(jnp.bfloat16)
    normed_in_grad = (
        outer_cols(query_grad, query_back)
        + outer_cols(key_grad, key_back)
        + outer_cols(value_grad, value_back)
    )
    input_part, input_gain_part = norm_backward(tokens_float, input_scale, normed_in_grad)
    tokens_gradient = (mixed_grad + input_part).astype(jnp.bfloat16)
    ffn_grads = (
        lax.psum_scatter(gate_part, "ctx", scatter_dimension=0, tiled=True),
        lax.psum_scatter(up_part, "ctx", scatter_dimension=0, tiled=True),
        lax.psum_scatter(down_part, "ctx", scatter_dimension=1, tiled=True),
    )
    attention_grads = (
        lax.psum_scatter(
            inner_rows(normed_in, query_grad), ("ctx", "fsdp"), scatter_dimension=0, tiled=True
        ),
        lax.psum_scatter(
            inner_rows(normed_in, key_grad), ("ctx", "fsdp"), scatter_dimension=0, tiled=True
        ),
        lax.psum_scatter(
            inner_rows(normed_in, value_grad), ("ctx", "fsdp"), scatter_dimension=0, tiled=True
        ),
        lax.psum_scatter(output_part, ("ctx", "fsdp"), scatter_dimension=0, tiled=True),
        lax.psum_scatter(input_gain_part, ("ctx", "fsdp"), scatter_dimension=0, tiled=True),
        lax.psum_scatter(attention_gain_part, ("ctx", "fsdp"), scatter_dimension=0, tiled=True),
        lax.psum_scatter(feedforward_gain_part, ("ctx", "fsdp"), scatter_dimension=0, tiled=True),
        lax.psum_scatter(output_gain_part, ("ctx", "fsdp"), scatter_dimension=0, tiled=True),
    )
    return (
        output,
        tokens_gradient,
        attention_grads[0],
        attention_grads[1],
        attention_grads[2],
        attention_grads[3],
        ffn_grads[0],
        ffn_grads[1],
        ffn_grads[2],
        attention_grads[4],
        attention_grads[5],
        attention_grads[6],
        attention_grads[7],
    )


def solution(mesh):
    placed = (
        P(("ctx", "fsdp"), None),
        P(("ctx", "fsdp"), None),
        P(("ctx", "fsdp"), None),
        P(("ctx", "fsdp"), None),
        P(("ctx", "fsdp"), None),
        P("ctx", "fsdp"),
        P("ctx", "fsdp"),
        P("fsdp", "ctx"),
        P(("ctx", "fsdp")),
        P(("ctx", "fsdp")),
        P(("ctx", "fsdp")),
        P(("ctx", "fsdp")),
        P(),
        P(("ctx", "fsdp"), None),
    )
    return jax.shard_map(
        shards,
        mesh=mesh,
        in_specs=placed,
        out_specs=(
            P(("ctx", "fsdp"), None),
            P(("ctx", "fsdp"), None),
            P(("ctx", "fsdp"), None),
            P(("ctx", "fsdp"), None),
            P(("ctx", "fsdp"), None),
            P(("ctx", "fsdp"), None),
            P("ctx", "fsdp"),
            P("ctx", "fsdp"),
            P("fsdp", "ctx"),
            P(("ctx", "fsdp")),
            P(("ctx", "fsdp")),
            P(("ctx", "fsdp")),
            P(("ctx", "fsdp")),
        ),
        check_vma=False,
    )
```

profile of v0, /device:TPU:0, one launch (start us, length us, event | category | flops | bytes accessed | tf_op | source)
XLA Modules:
  0.0 2533.5 jit_solution(2754236725002149494)
XLA Ops:
  11.4 68.4 %all-reduce.14 = (bf16[640]{0:T(1024)(128)(2,1)S(1)}, bf16[640]{0:T(1024)(128)(2,1)S(1)}, bf16[640]{0:T(1024)(128)(2,1)S(1)}, bf16[640]{0:T(1024)(128)(2,1)S(1)}) all-reduce(bf16[640]{0:T(1024)(128)(2,1)S(1)} %dynamic-update-slice, bf16[640]{0:T(1024)(128)(2,1)S(1)} %dynamic-update-slice.1, ...), channel_id=1, replica_groups=mesh['ctx'=8,'fsdp'=16] {'ctx','fsdp'}, use_global_device_ids=true, to_apply=%add | all-reduce | flops 2560 | bytes 10240
  80.8 125.9 %all-gather.27.cloned.1.call-done = bf16[128,5,1024]{2,1,0:T(8,128)(2,1)} async-done(((bf16[1,5,1024]{2,1,0:T(8,128)(2,1)}), bf16[128,5,1024]{2,1,0:T(8,128)(2,1)}) %all-gather.27.cloned.1.call-update) | async-done | bytes 1310736 | tf_op jit(solution)/shard_map/all_gather | solution.py:89
  211.5 175.2 %all-gather.2 = bf16[128,5,256]{2,1,0:T(8,128)(2,1)S(1)} all-gather(bf16[1,5,256]{2,1,0:T(8,128)(2,1)S(1)} %bitcast.184), channel_id=1, replica_groups=mesh['ctx'=8,'fsdp'=16] {'ctx','fsdp'}, dimensions={0}, use_global_device_ids=true | all-gather | bytes 330240 | tf_op jit(solution)/shard_map/all_gather | solution.py:91
  386.9 171.9 %all-gather.1 = bf16[128,5,256]{2,1,0:T(8,128)(2,1)S(1)} all-gather(bf16[1,5,256]{2,1,0:T(8,128)(2,1)S(1)} %bitcast.182), channel_id=1, replica_groups=mesh['ctx'=8,'fsdp'=16] {'ctx','fsdp'}, dimensions={0}, use_global_device_ids=true | all-gather | bytes 330240 | tf_op jit(solution)/shard_map/all_gather | solution.py:90
  559.4 35.8 %all_gather.84 = bf16[1024,256]{1,0:T(8,128)(2,1)S(1)} all-gather(bf16[128,256]{1,0:T(8,128)(2,1)S(1)} %convolution_convert_fusion.2), channel_id=1, replica_groups=mesh['ctx'=8,'fsdp'=16] {'ctx'}, dimensions={0}, use_global_device_ids=true | all-gather | bytes 589824 | tf_op jit(solution)/shard_map/all_gather | solution.py:202
  595.5 36.0 %all_gather.82 = bf16[1024,256]{1,0:T(8,128)(2,1)S(1)} all-gather(bf16[128,256]{1,0:T(8,128)(2,1)S(1)} %convolution_convert_fusion.3), channel_id=1, replica_groups=mesh['ctx'=8,'fsdp'=16] {'ctx'}, dimensions={0}, use_global_device_ids=true | all-gather | bytes 589824 | tf_op jit(solution)/shard_map/all_gather | solution.py:201
  631.5 4.4 copy.81
  638.8 40.5 %while.34 = (s32[]{:T(128)}, f32[4,2048,256]{2,1,0:T(8,128)}, f32[4,2048]{1,0:T(4,128)}, f32[4,2048]{1,0:T(4,128)S(1)}, bf16[4,2048,256]{2,1,0:T(8,128)(2,1)}, /...) while((s32[]{:T(128)}, f32[4,2048,256]{2,1,0:T(8,128)}, ...), condition=%wide.region_6.7_spmd.clone, body=%wide.region_3.6_spmd.clone.sunk | while | flops 2166353920 | bytes 29440124 | solution.py:207
  643.4 4.0 fusion.184
  648.9 3.4 fusion.183
  653.6 4.0 fusion.184
  663.7 4.0 fusion.184
  669.2 3.4 fusion.183
  673.8 4.0 fusion.184
  679.3 9.2 all_to_all.15
  688.5 3.5 all-to-all-start.1
  692.0 8.7 copy.46
  700.7 5.4 copy.76
  706.1 5.8 copy.47
  711.9 5.7 all-to-all-start
  718.9 95.0 %all-to-all-done = f32[16,128,1024]{1,2,0:T(8,128)} async-done(((f32[16,128,1024]{1,2,0:T(8,128)}), f32[16,128,1024]{1,2,0:T(8,128)}, u32[]{:S(2)}, u32[]{:S(2)}) %all-to-all-start) | async-done | bytes 8388640 | tf_op jit(solution)/shard_map/all_to_all | solution.py:211
  813.9 4.0 fusion.58
  818.3 155.3 %all-gather.17.cloned.1.call-done = bf16[1024,640]{1,0:T(8,128)(2,1)} async-done(((bf16[8,640]{1,0:T(8,128)(2,1)}), bf16[1024,640]{1,0:T(8,128)(2,1)}) %all-gather.17.cloned.1.call-update) | async-done | bytes 1310736 | tf_op jit(solution)/shard_map/all_gather | solution.py:92
  976.5 34.9 %all_gather.89 = bf16[640,128]{1,0:T(8,128)(2,1)S(1)} all-gather(bf16[80,128]{1,0:T(8,128)(2,1)S(1)} %copy-done.19), channel_id=1, replica_groups=mesh['ctx'=8,'fsdp'=16] {'ctx'}, dimensions={0}, use_global_device_ids=true | all-gather | bytes 184320 | tf_op jit(solution)/shard_map/all_gather | solution.py:102
  1011.4 34.6 %all_gather.90 = bf16[640,128]{1,0:T(8,128)(2,1)S(1)} all-gather(bf16[80,128]{1,0:T(8,128)(2,1)S(1)} %copy-done.20), channel_id=1, replica_groups=mesh['ctx'=8,'fsdp'=16] {'ctx'}, dimensions={0}, use_global_device_ids=true | all-gather | bytes 184320 | tf_op jit(solution)/shard_map/all_gather | solution.py:103
  1046.0 34.4 %all_gather.91 = bf16[128,640]{0,1:T(8,128)(2,1)S(1)} all-gather(bf16[128,80]{0,1:T(8,128)(2,1)S(1)} %copy-done.18), channel_id=1, replica_groups=mesh['ctx'=8,'fsdp'=16] {'ctx'}, dimensions={1}, use_global_device_ids=true | all-gather | bytes 184320 | tf_op jit(solution)/shard_map/all_gather | solution.py:104
  1089.0 70.3 %reduce-scatter.9.cloned.1.call-done = f32[128,640]{1,0:T(8,128)} async-done(((f32[2048,640]{1,0:T(8,128)}), f32[128,640]{1,0:T(8,128)}) %reduce-scatter.9.cloned.1.call-update) | async-done | bytes 327696 | tf_op jit(solution)/shard_map/reduce_scatter | solution.py:248
  1164.2 34.7 %all_gather.94 = bf16[128,640]{0,1:T(8,128)(2,1)S(1)} all-gather(bf16[128,80]{0,1:T(8,128)(2,1)S(1)} %copy-done.18), channel_id=1, replica_groups=mesh['ctx'=8,'fsdp'=16] {'ctx'}, dimensions={1}, use_global_device_ids=true | all-gather | bytes 184320 | tf_op jit(solution)/shard_map/all_gather | solution.py:104
  1198.9 34.4 %all_gather.95 = bf16[640,128]{1,0:T(8,128)(2,1)S(1)} all-gather(bf16[80,128]{1,0:T(8,128)(2,1)S(1)} %copy-done.19), channel_id=1, replica_groups=mesh['ctx'=8,'fsdp'=16] {'ctx'}, dimensions={0}, use_global_device_ids=true | all-gather | bytes 184320 | tf_op jit(solution)/shard_map/all_gather | solution.py:102
  1233.3 45.5 %all_gather.96 = bf16[640,128]{1,0:T(8,128)(2,1)S(1)} all-gather(bf16[80,128]{1,0:T(8,128)(2,1)S(1)} %copy-done.20), channel_id=1, replica_groups=mesh['ctx'=8,'fsdp'=16] {'ctx'}, dimensions={0}, use_global_device_ids=true | all-gather | bytes 184320 | tf_op jit(solution)/shard_map/all_gather | solution.py:103
  1278.9 3.5 multiply_convert_fusion.1
  1287.2 71.4 %reduce-scatter.11.cloned.1.call-done = f32[128,640]{1,0:T(8,128)} async-done(((f32[2048,640]{1,0:T(8,128)}), f32[128,640]{1,0:T(8,128)}) %reduce-scatter.11.cloned.1.call-update) | async-done | bytes 327696 | tf_op jit(solution)/shard_map/reduce_scatter | solution.py:266
  1362.5 192.6 %all-gather.23.cloned.1.call-done = bf16[1024,640]{1,0:T(8,128)(2,1)} async-done(((bf16[8,640]{1,0:T(8,128)(2,1)}), bf16[1024,640]{1,0:T(8,128)(2,1)}) %all-gather.23.cloned.1.call-update) | async-done | bytes 1310736 | tf_op jit(solution)/shard_map/all_gather | solution.py:92
  1557.8 18.1 all_gather.97
  1576.4 27.3 %all_gather.100 = f32[2048,4]{1,0:T(8,128)S(1)} all-gather(f32[128,4]{1,0:T(8,128)S(1)} %reduce_sum.210), channel_id=1, replica_groups=mesh['ctx'=8,'fsdp'=16] {'fsdp'}, dimensions={0}, use_global_device_ids=true | all-gather | bytes 34816 | tf_op jit(solution)/shard_map/all_gather | solution.py:302
  1604.0 4.4 copy.80
  1608.4 93.5 %while.35 = (s32[]{:T(128)}, f32[4,2048,256]{1,2,0:T(8,128)}, f32[4,1024,256]{2,1,0:T(8,128)}, f32[4,1024,256]{2,1,0:T(8,128)}, bf16[4,2048,256]{2,1,0:T(8,128)(...) while((s32[]{:T(128)}, f32[4,2048,256]{1,2,0:T(8,128)}, ...), condition=%wide.region_20.21_spmd.clone, body=%wide.region_19.20_spmd.clone.sunk | while | flops 5405147136 | bytes 72962224 | solution.py:305
  1611.3 5.9 multiply_convert_fusion.6
  1617.1 4.0 fusion.199
  1621.2 3.7 fusion.197
  1624.8 3.6 fusion.198
  1634.7 5.9 multiply_convert_fusion.6
  1640.5 4.1 fusion.199
  1644.6 3.7 fusion.197
  1648.3 3.5 fusion.198
  1658.0 5.9 multiply_convert_fusion.6
  1663.9 4.1 fusion.199
  1667.9 3.7 fusion.197
  1671.6 3.5 fusion.198
  1681.3 5.9 multiply_convert_fusion.6
  1687.2 4.1 fusion.199
  1691.3 3.7 fusion.197
  1694.9 3.5 fusion.198
  1701.9 3.6 reduce_sum.212
  1705.5 3.6 reduce_sum.211
  1712.6 62.9 %reduce-scatter.17.cloned.1.call-done = f32[128,256]{1,0:T(8,128)} async-done(((f32[1024,256]{1,0:T(8,128)}), f32[128,256]{1,0:T(8,128)}) %reduce-scatter.17.cloned.1.call-update) | async-done | bytes 131088 | tf_op jit(solution)/shard_map/reduce_scatter | solution.py:321
  1777.6 72.6 %reduce-scatter.15.cloned.1.call-done = f32[128,256]{1,0:T(8,128)} async-done(((f32[1024,256]{1,0:T(8,128)}), f32[128,256]{1,0:T(8,128)}) %reduce-scatter.15.cloned.1.call-update) | async-done | bytes 131088 | tf_op jit(solution)/shard_map/reduce_scatter | solution.py:320
  1852.4 97.2 %reduce-scatter.13.cloned.1.call-done = f32[128,1024]{0,1:T(8,128)} async-done(((f32[2048,1024]{0,1:T(8,128)}), f32[128,1024]{0,1:T(8,128)}) %reduce-scatter.13.cloned.1.call-update) | async-done | bytes 524304 | tf_op jit(solution)/shard_map/reduce_scatter | solution.py:316
  1953.0 3.8 fusion.131
  1961.4 175.9 %all-gather.4 = bf16[128,5,256]{2,1,0:T(8,128)(2,1)S(1)} all-gather(bf16[1,5,256]{2,1,0:T(8,128)(2,1)S(1)} %bitcast.183), channel_id=1, replica_groups=mesh['ctx'=8,'fsdp'=16] {'ctx','fsdp'}, dimensions={0}, use_global_device_ids=true | all-gather | bytes 330240 | tf_op jit(solution)/shard_map/all_gather | solution.py:90
  2137.4 172.7 %all-gather.5 = bf16[128,5,256]{2,1,0:T(8,128)(2,1)S(1)} all-gather(bf16[1,5,256]{2,1,0:T(8,128)(2,1)S(1)} %bitcast.185), channel_id=1, replica_groups=mesh['ctx'=8,'fsdp'=16] {'ctx','fsdp'}, dimensions={0}, use_global_device_ids=true | all-gather | bytes 330240 | tf_op jit(solution)/shard_map/all_gather | solution.py:91
  2314.2 64.2 %all-reduce.12 = (f32[640]{0:T(1024)S(1)}, f32[640]{0:T(1024)S(1)}, f32[640]{0:T(1024)S(1)}, f32[640]{0:T(1024)S(1)}) all-reduce(f32[640]{0:T(1024)S(1)} %get-tuple-element.359, f32[640]{0:T(1024)S(1)} %copy-done.28, f32[640]{0:T(1024)S(1)} %copy-done.29, ...), channel_id=14, replica_groups=mesh['ctx'=8,'fsdp'=16] {'ctx','fsdp'}, use_global_device_ids=true, to_apply=%region_35.36.clone | all-reduce | flops 2560 | bytes 20480
  2385.7 68.0 %reduce-scatter.19.cloned.1.call-done = f32[80,128]{1,0:T(8,128)} async-done(((f32[640,128]{1,0:T(8,128)}), f32[80,128]{1,0:T(8,128)}) %reduce-scatter.19.cloned.1.call-update) | async-done | bytes 40976 | tf_op jit(solution)/shard_map/reduce_scatter | solution.py:333
  2453.7 73.0 %reduce-scatter.21.cloned.1.call-done = f32[80,128]{1,0:T(8,128)} async-done(((f32[640,128]{1,0:T(8,128)}), f32[80,128]{1,0:T(8,128)}) %reduce-scatter.21.cloned.1.call-update) | async-done | bytes 40976 | tf_op jit(solution)/shard_map/reduce_scatter | solution.py:334
  (227 shorter events, 113.3 us)
Async XLA Ops:
  7.2 204.3 %copy-start.25 = (bf16[5,256]{1,0:T(8,128)(2,1)S(1)}, bf16[5,256]{1,0:T(8,128)(2,1)}, u32[]{:S(2)}) copy-start(bf16[5,256]{1,0:T(8,128)(2,1)} %param.21) | copy-start | bytes 7684
  7.2 379.7 %copy-start.23 = (bf16[5,256]{1,0:T(8,128)(2,1)S(1)}, bf16[5,256]{1,0:T(8,128)(2,1)}, u32[]{:S(2)}) copy-start(bf16[5,256]{1,0:T(8,128)(2,1)} %param.20) | copy-start | bytes 7684
  7.2 199.5 %all-gather.27.cloned.1.call-start = ((), (), s32[]{:S(2)}) async-start(), calls=%async_computation.25 | async-start | bytes 2113536 | tf_op jit(solution)/shard_map/all_gather | solution.py:89
  7.9 623.6 %all-gather.15.cloned.1.call-start = ((), (), s32[]{:S(2)}) async-start(), calls=%async_computation.11 | async-start | bytes 4456448 | tf_op jit(solution)/shard_map/all_gather | solution.py:199
  79.7 479.2 %copy-start.30 = (s32[16]{0:T(128)S(1)}, s32[16]{0:T(128)}, u32[]{:S(2)}) copy-start(s32[16]{0:T(128)} %param.30) | copy-start | bytes 196
  80.8 478.4 %copy-start.2 = (bf16[128,640]{1,0:T(8,128)(2,1)S(1)}, bf16[128,640]{1,0:T(8,128)(2,1)}, u32[]{:S(2)}) copy-start(bf16[128,640]{1,0:T(8,128)(2,1)} %param.18) | copy-start | bytes 491524
  80.8 514.5 %copy-start.21 = (f32[128]{0:T(128)}, f32[128]{0:T(128)S(1)}, u32[]{:S(2)}) copy-start(f32[128]{0:T(128)S(1)} %add_rsqrt_fusion.3) | copy-start | bytes 1540
  80.8 514.4 %copy-start.16 = (f32[640]{0:T(1024)}, f32[640]{0:T(1024)S(1)}, u32[]{:S(2)}) copy-start(f32[640]{0:T(1024)S(1)} %convert_add_fusion.5) | copy-start | bytes 7684
  688.5 23.4 all-to-all-start.1
  711.9 102.0 %all-to-all-start = ((f32[16,128,1024]{1,2,0:T(8,128)}), f32[16,128,1024]{1,2,0:T(8,128)}, u32[]{:S(2)}, u32[]{:S(2)}) async-start(f32[16,128,1024]{1,2,0:T(8,128)} %copy.47), calls=%async_computation | async-start | bytes 16777216 | tf_op jit(solution)/shard_map/all_to_all | solution.py:211
  717.6 256.0 %all-gather.17.cloned.1.call-start = ((), (), s32[]{:S(2)}) async-start(), calls=%async_computation.12 | async-start | bytes 1320960 | tf_op jit(solution)/shard_map/all_gather | solution.py:92
  718.3 362.0 %all-gather.19.cloned.1.call-start = ((), (), s32[]{:S(2)}) async-start(), calls=%async_computation.13 | async-start | bytes 2785280 | tf_op jit(solution)/shard_map/all_gather | solution.py:243
  817.9 158.5 %copy-start.19 = (bf16[80,128]{1,0:T(8,128)(2,1)S(1)}, bf16[80,128]{1,0:T(8,128)(2,1)}, u32[]{:S(2)}) copy-start(bf16[80,128]{1,0:T(8,128)(2,1)} %param.23) | copy-start | bytes 61444
  818.0 193.4 %copy-start.20 = (bf16[80,128]{1,0:T(8,128)(2,1)S(1)}, bf16[80,128]{1,0:T(8,128)(2,1)}, u32[]{:S(2)}) copy-start(bf16[80,128]{1,0:T(8,128)(2,1)} %param.24) | copy-start | bytes 61444
  818.0 228.0 %copy-start.18 = (bf16[128,80]{0,1:T(8,128)(2,1)S(1)}, bf16[128,80]{0,1:T(8,128)(2,1)}, u32[]{:S(2)}) copy-start(bf16[128,80]{0,1:T(8,128)(2,1)} %param.25) | copy-start | bytes 61444
  976.4 182.9 %reduce-scatter.9.cloned.1.call-start = ((), (), s32[]{:S(2)}) async-start(), calls=%async_computation.14 | async-start | bytes 5570560 | tf_op jit(solution)/shard_map/reduce_scatter | solution.py:248
  1080.4 2.7 copy-start
  1085.0 0.8 copy-start.7
  1089.0 71.5 %copy-start.13 = (bf16[128,640]{1,0:T(8,128)(2,1)S(1)}, bf16[128,640]{1,0:T(8,128)(2,1)}, u32[]{:S(2)}) copy-start(bf16[128,640]{1,0:T(8,128)(2,1)} %param.31) | copy-start | bytes 491524
  1089.0 189.9 %all-gather.21.cloned.1.call-start = ((), (), s32[]{:S(2)}) async-start(), calls=%async_computation.15 | async-start | bytes 2785280 | tf_op jit(solution)/shard_map/all_gather | solution.py:258
  1164.2 194.5 %reduce-scatter.11.cloned.1.call-start = ((), (), s32[]{:S(2)}) async-start(), calls=%async_computation.16 | async-start | bytes 5570560 | tf_op jit(solution)/shard_map/reduce_scatter | solution.py:266
  1282.3 0.8 copy-start.11
  1282.4 1.6 copy-start.9
  1287.2 267.9 %all-gather.23.cloned.1.call-start = ((), (), s32[]{:S(2)}) async-start(), calls=%async_computation.17 | async-start | bytes 1320960 | tf_op jit(solution)/shard_map/all_gather | solution.py:92
  1362.3 213.9 %copy-start.5 = (f32[128,640]{1,0:T(8,128)}, f32[128,640]{1,0:T(8,128)S(1)}, u32[]{:S(2)}) copy-start(f32[128,640]{1,0:T(8,128)S(1)} %get-tuple-element.415) | copy-start | bytes 983044
  1362.4 241.5 %all-gather.25.cloned.1.call-start = ((), (), s32[]{:S(2)}) async-start(), calls=%async_computation.18 | async-start | bytes 4456448 | tf_op jit(solution)/shard_map/all_gather | solution.py:301
  1557.7 217.8 %reduce-scatter.17.cloned.1.call-start = ((), (), s32[]{:S(2)}) async-start(), calls=%async_computation.21 | async-start | bytes 1179648 | tf_op jit(solution)/shard_map/reduce_scatter | solution.py:321
  1608.4 2.8 copy-start.4
  1631.8 2.8 copy-start.4
  1655.2 2.8 copy-start.4
  1678.5 2.8 copy-start.4
  1705.5 144.8 %reduce-scatter.15.cloned.1.call-start = ((), (), s32[]{:S(2)}) async-start(), calls=%async_computation.20 | async-start | bytes 1179648 | tf_op jit(solution)/shard_map/reduce_scatter | solution.py:320
  1709.2 240.5 %reduce-scatter.13.cloned.1.call-start = ((), (), s32[]{:S(2)}) async-start(), calls=%async_computation.19 | async-start | bytes 8912896 | tf_op jit(solution)/shard_map/reduce_scatter | solution.py:316
  1709.2 66.3 %copy-start.3 = (bf16[128,640]{1,0:T(8,128)(2,1)S(1)}, bf16[128,640]{1,0:T(8,128)(2,1)}, u32[]{:S(2)}) copy-start(bf16[128,640]{1,0:T(8,128)(2,1)} %param.18) | copy-start | bytes 491524
  1709.2 66.3 %copy-start.17 = (f32[640]{0:T(1024)S(1)}, f32[640]{0:T(1024)}, u32[]{:S(2)}) copy-start(f32[640]{0:T(1024)} %copy-done.16) | copy-start | bytes 7684
  1709.2 66.3 %copy-start.22 = (f32[128]{0:T(128)S(1)}, f32[128]{0:T(128)}, u32[]{:S(2)}) copy-start(f32[128]{0:T(128)} %copy-done.21) | copy-start | bytes 1540
  1709.7 600.6 %all-gather.29.cloned.1.call-start = ((), (), s32[]{:S(2)}) async-start(), calls=%async_computation.26 | async-start | bytes 2113536 | tf_op jit(solution)/shard_map/all_gather | solution.py:89
  1710.5 671.1 %all-reduce.17.cloned.1.call-start = ((), (), s32[]{:S(2)}) async-start(), calls=%async_computation.27 | async-start | bytes 13107200
  1852.4 100.7 %copy-start.8 = (bf16[2048,128]{1,0:T(8,128)(2,1)S(1)}, bf16[2048,128]{1,0:T(8,128)(2,1)}, u32[]{:S(2)}) copy-start(bf16[2048,128]{1,0:T(8,128)(2,1)} %copy-done.7) | copy-start | bytes 1572868
  1952.7 4.2 copy-start.1
  1952.8 432.9 %reduce-scatter.23.cloned.1.call-start = ((), (), s32[]{:S(2)}) async-start(), calls=%async_computation.24 | async-start | bytes 368640 | tf_op jit(solution)/shard_map/reduce_scatter | solution.py:335
  1956.8 2.9 copy-start.10
  1956.8 4.5 copy-start.24
  1956.8 180.6 %copy-start.26 = (bf16[5,256]{1,0:T(8,128)(2,1)S(1)}, bf16[5,256]{1,0:T(8,128)(2,1)}, u32[]{:S(2)}) copy-start(bf16[5,256]{1,0:T(8,128)(2,1)} %param.21) | copy-start | bytes 7684
  1956.8 496.8 %reduce-scatter.19.cloned.1.call-start = ((), (), s32[]{:S(2)}) async-start(), calls=%async_computation.22 | async-start | bytes 368640 | tf_op jit(solution)/shard_map/reduce_scatter | solution.py:333
  1959.7 567.0 %reduce-scatter.21.cloned.1.call-start = ((), (), s32[]{:S(2)}) async-start(), calls=%async_computation.23 | async-start | bytes 368640 | tf_op jit(solution)/shard_map/reduce_scatter | solution.py:334
  1961.3 351.7 %copy-start.12 = (f32[128,1024]{0,1:T(8,128)S(1)}, f32[128,1024]{0,1:T(8,128)}, u32[]{:S(2)}) copy-start(f32[128,1024]{0,1:T(8,128)} %reduce-scatter.13.cloned.1.call-done) | copy-start | bytes 1572868
  1961.3 352.2 %copy-start.15 = (f32[128,256]{1,0:T(8,128)S(1)}, f32[128,256]{1,0:T(8,128)}, u32[]{:S(2)}) copy-start(f32[128,256]{1,0:T(8,128)} %reduce-scatter.15.cloned.1.call-done) | copy-start | bytes 393220
  2137.4 176.4 %copy-start.14 = (f32[128,256]{1,0:T(8,128)S(1)}, f32[128,256]{1,0:T(8,128)}, u32[]{:S(2)}) copy-start(f32[128,256]{1,0:T(8,128)} %reduce-scatter.17.cloned.1.call-done) | copy-start | bytes 393220
  2310.3 4.0 copy-start.27
  2310.3 4.0 copy-start.28
  2310.3 4.0 copy-start.29
  2310.3 70.5 %copy-start.6 = (f32[128,640]{1,0:T(8,128)S(1)}, f32[128,640]{1,0:T(8,128)}, u32[]{:S(2)}) copy-start(f32[128,640]{1,0:T(8,128)} %copy-done.5) | copy-start | bytes 983044
Sparse Core Ops, SparseCore 0:
  9.8 196.9 all-gather.26
  211.6 35.9 all-gather.14
  720.2 253.4 all-gather.16
  976.6 34.6 all-gather.18
  1089.1 70.2 reduce-scatter.8
  1164.3 33.9 all-gather.20
  1287.3 71.3 reduce-scatter.10
  1362.6 192.4 all-gather.22
  1557.8 42.3 all-gather.24
  1705.6 69.8 reduce-scatter.16
  1779.5 70.6 reduce-scatter.14
  1852.5 97.0 reduce-scatter.12
  1951.3 193.0 all-gather.28
  2149.9 158.4 all-reduce.16
  2312.3 68.3 reduce-scatter.22
  2384.6 68.9 reduce-scatter.18
  2457.6 68.9 reduce-scatter.20
where the time goes:
time: 2540 us; the launch traced here: 2530 us
  blocking collectives  1170 us (46%)
  waiting for transfers between devices  1090 us (43%)
  matrix products  150 us (6%)
  local copies, waits for them, and re-layouts  69.9 us (3%)
  other arithmetic  27.9 us (1%)
    all_gather x2, waiting for transfers between devices, fetch_attention(): lax.all_gather(output_weight, ('ctx', 'fsdp'), axis=0, tiled=True)  348 us
    all_gather x2, blocking collectives, fetch_attention(): lax.all_gather(value_weight, ('ctx', 'fsdp'), axis=0, tiled=True)  348 us
    all_gather x2, blocking collectives, fetch_attention(): lax.all_gather(key_weight, ('ctx', 'fsdp'), axis=0, tiled=True)  348 us
    unnamed x2, blocking collectives  133 us
    all_gather x2, waiting for transfers between devices, fetch_attention(): lax.all_gather(query_weight, ('ctx', 'fsdp'), axis=0, tiled=True)  126 us
    reduce_scatter x1, waiting for transfers between devices, shards(): lax.psum_scatter(join_query(query_parts), 'fsdp', scatter_dimension=0, ti...  97.2 us
    all_to_all x1, waiting for transfers between devices, shards(): lax.all_to_all(join_query(summed).reshape(fsdp_size, own_rows, H * HD), '...  95 us
    all_gather x2, blocking collectives, fetch_feedforward(): lax.all_gather(up_weight, 'ctx', axis=0, tiled=True)  80.1 us
  transfers between devices with their start and end apart: 19, of which 11 were waited for; matrix products, arithmetic and copies ran while one was open for 3% of the time, Pallas kernels for 0%

commit v1 on v0

v1 whole, which is shorter than its diff:
```python
import itertools
import math

import jax
import jax.numpy as jnp
from jax import lax
from jax.experimental import pallas as pl
from jax.experimental.pallas import tpu as pltpu
from jax.sharding import PartitionSpec as P

MESH = pl.DeviceIdType.MESH
F32, BF = jnp.float32, jnp.bfloat16
ALL = slice(None)
D, H, HD, FF = 640, 4, 256, 2048
ROWS = 128
SOFTCAP = 50.0
EPS = 1e-6
MASKED = -1e30
SCORE = 1.0 / (math.sqrt(HD) * SOFTCAP)
EXPO = SOFTCAP * math.log2(math.e)
ORDERS = ((0, 1, 2), (1, 2, 0), (2, 0, 1))
KV_ROWS = ((0, 48), (48, 48), (96, 32))
VMEM_LIMIT = 62 * 2**20


def nn(a, b):
    return lax.dot_general(a, b, (((1,), (0,)), ((), ())), preferred_element_type=F32)


def nt(a, b):
    return lax.dot_general(a, b, (((1,), (1,)), ((), ())), preferred_element_type=F32)


def tn(a, b):
    return lax.dot_general(a, b, (((0,), (0,)), ((), ())), preferred_element_type=F32)


def nt_exact(a, b):
    return lax.dot_general(
        a, b, (((1,), (1,)), ((), ())), precision=lax.Precision.HIGHEST, preferred_element_type=F32
    )


def nn_exact(a, b):
    return lax.dot_general(
        a, b, (((1,), (0,)), ((), ())), precision=lax.Precision.HIGHEST, preferred_element_type=F32
    )


def iota(shape, dim):
    return lax.broadcasted_iota(jnp.int32, shape, dim)


def rms_scale(v):
    return lax.rsqrt(jnp.mean(v * v, axis=-1, keepdims=True) + EPS)


def norm_forward(v, gain):
    return v * rms_scale(v) * (1.0 + gain)


def norm_backward(v, gain, upstream):
    scale = rms_scale(v)
    normed = v * scale
    gain_part = jnp.sum(upstream * normed, axis=0, keepdims=True)
    inner = upstream * (1.0 + gain)
    return scale * (inner - normed * jnp.mean(inner * normed, axis=-1, keepdims=True)), gain_part


def coords():
    c, f = lax.axis_index("ctx"), lax.axis_index("fsdp")
    return ((c % 2) * 2 + (f // 2) % 2, c // 2, f // 4, f % 2)


def device(x, y, z, core):
    return (y * 2 + x // 2, z * 4 + (x % 2) * 2 + core)


def step(co, d, s):
    co = list(co)
    co[d] = (co[d] + s) % 4
    return co


class Copies:
    def __init__(self, co, ssem, rsem):
        self.co, self.ssem, self.rsem = co, ssem, rsem
        self.count, self.started = 0, []

    def go(self, src, dst, to):
        copy = pltpu.make_async_remote_copy(
            src_ref=src,
            dst_ref=dst,
            send_sem=self.ssem.at[self.count],
            recv_sem=self.rsem.at[self.count],
            device_id=device(*to),
            device_id_type=MESH,
        )
        copy.start()
        self.count += 1
        self.started.append(copy)
        return copy

    def line(self, src, dst, d, s):
        return self.go(src, dst, step(self.co, d, s))

    def sibling(self, src, dst):
        x, y, z, core = self.co
        return self.go(src, dst, (x, y, z, 1 - core))

    def sent(self, copy):
        copy.wait_send()
        self.started = [c for c in self.started if c is not copy]

    def drain(self):
        for copy in self.started:
            copy.wait_send()


def greet(co):
    sem = pltpu.get_barrier_semaphore()
    partners = [step(co, d, s) for d in range(3) for s in (1, 2, 3)]
    partners.append((co[0], co[1], co[2], 1 - co[3]))
    for partner in partners:
        pl.semaphore_signal(sem, inc=1, device_id=device(*partner), device_id_type=MESH)
    return lambda: pl.semaphore_wait(sem, len(partners))


class Gather:
    def __init__(self, copies, view, parts):
        self.copies, self.view, self.parts, self.co = copies, view, parts, copies.co
        self.open = {p: [] for p in parts}
        self.edge = {}

    def send(self, p, pos, d, s):
        ref = self.view(p, pos)
        return self.copies.line(ref, ref, d, s)

    def place(self, p, n):
        pos = list(self.co[:3])
        for d in ORDERS[p][:n]:
            pos[d] = ALL
        return pos

    def phase(self, n, forward=False):
        for p in self.parts:
            d = ORDERS[p][n]
            for s in (1, 3) if forward else (1, 3, 2):
                copy = self.send(p, self.place(p, n), d, s)
                if forward:
                    self.edge[p, s] = copy
                else:
                    self.open[p].append(copy)

    def forward(self, halves):
        for p in self.parts:
            a, d = ORDERS[p][0], ORDERS[p][2]
            for k, s in enumerate((1, 3)):
                self.edge[p, s].wait_recv()
                pos = self.place(p, 2)
                pos[d] = (self.co[d] - s) % 4
                pos[a] = halves(a, k)
                self.open[p].append(self.send(p, pos, d, s))

    def wait(self, p):
        for copy in self.open[p]:
            copy.wait_recv()
        self.open[p] = []

    def wait_all(self):
        for p in self.parts:
            self.wait(p)


class KeyGather:
    def __init__(self, copies, buf):
        self.copies, self.buf, self.cp = copies, buf, {}

    def view(self, p, pos):
        return self.buf.at[pos[0], pos[1], pos[2], pl.ds(*KV_ROWS[p]), :]

    def send(self, p, tag, sel, d, s, at=0):
        pos = [0, 0, 0]
        for dim, v in sel.items():
            pos[dim] = v
        pos[d] = at
        src = self.view(p, pos)
        pos[d] = (at - s) % 4
        self.cp[p, tag, s] = self.copies.line(src, self.view(p, pos), d, s)

    def wait(self, p, tag, steps=(1, 2, 3)):
        for s in steps:
            self.cp[p, tag, s].wait_recv()

    def start(self):
        for n, tag in enumerate(("1", "2A", "3A")):
            for p in range(3):
                for s in (1, 3, 2):
                    self.send(p, tag, {}, ORDERS[p][n], s)

    def mid(self):
        for p in range(3):
            a, b, c = ORDERS[p]
            self.wait(p, "1")
            for s in (1, 3, 2):
                self.send(p, "2B", {a: pl.ds(1, 3)}, b, s)
        for p in range(3):
            a, b, c = ORDERS[p]
            for s in (1, 3, 2):
                self.send(p, "3B", {a: pl.ds(1, 3)}, c, s)

    def last(self):
        for p in range(3):
            a, b, c = ORDERS[p]
            self.wait(p, "2A")
            self.wait(p, "2B")
            for s in (1, 3):
                self.send(p, "3C", {a: ALL, b: pl.ds(1, 3)}, c, s)

    def forward(self):
        for p in range(3):
            a, b, c = ORDERS[p]
            for k, s in enumerate((1, 3)):
                self.wait(p, "3C", (s,))
                self.send(p, "3D", {a: pl.ds(2 * k, 2), b: pl.ds(1, 3)}, c, s, at=(-s) % 4)

    def wait_edges(self):
        for p in range(3):
            self.wait(p, "3A", (1, 3))
            self.wait(p, "3B", (1, 3))

    def wait_opposite(self):
        for p in range(3):
            self.wait(p, "3A", (2,))
            self.wait(p, "3B", (2,))
            self.wait(p, "3D", (1, 3))


class Scatter:
    def __init__(self, copies, p, views, targets, r, s):
        self.copies, self.views, self.targets, self.r, self.s = copies, views, targets, r, s
        self.axes = ORDERS[p][::-1]
        self.open = []

    def send(self, n, steps=(1, 3, 2)):
        d = self.axes[n]
        for s in steps:
            ref, index = self.views[n](self.targets(d, s))
            self.open.append(self.copies.line(ref.at[index], self.r[n].at[s - 1], d, s))

    def total(self, n, write):
        for copy in self.open:
            copy.wait_recv()
        self.open = []
        ref, index = self.views[n](self.targets(self.axes[n], 0))
        index = index + (ALL,) * (len(ref.shape) - len(index))
        lead = self.r[n].shape[1:-2]
        for at in itertools.product(*(range(size) for size in lead)):
            left = list(at)
            full = tuple(left.pop(0) if i is ALL and left else i for i in index)
            got = ref[full].astype(F32)
            for s in range(3):
                got = got + self.r[n][(s,) + at].astype(F32)
            write(at, got)

    def fold(self, n):
        def write(at, got):
            self.s[n][at] = got.astype(BF)

        self.total(n, write)


class Everywhere:
    def __init__(self, copies, have, got):
        self.copies, self.have, self.got, self.open = copies, have, got, []

    def send(self, n):
        if n == 0:
            self.open = [self.copies.sibling(self.have.at[0], self.got.at[0, 0])]
        else:
            self.open = [
                self.copies.line(self.have.at[n], self.got.at[n, s - 1], n - 1, s) for s in (1, 3, 2)
            ]

    def fold(self, n):
        total = self.have[n].astype(F32)
        for i, copy in enumerate(self.open):
            copy.wait_recv()
        for i in range(len(self.open)):
            total = total + self.got[n, i].astype(F32)
        self.have[n + 1] = total.astype(self.have.dtype)


def weight_view(buf, core, lanes):
    def view(p, pos):
        x, y, z = pos
        hi, lo = (ALL, ALL) if x is ALL else (x // 2, x % 2)
        return buf.at[core, y, hi, z, lo, :, lanes[p]]

    return view


def ffn_view(buf):
    def view(p, pos):
        x, y, z = pos
        if isinstance(x, tuple):
            hi, lo = x[0], ALL
        else:
            hi, lo = (ALL, ALL) if x is ALL else (x // 2, x % 2)
        return buf.at[p, z, lo, y, hi]

    return view


def ffn_halves(a, k):
    return (k,) if a == 0 else pl.ds(2 * k, 2)


def absolute(co):
    return lambda d, s: (co[d] + s) % 4


def ffn_scatter_views(buf, s, p):
    if p == 0:
        return (
            lambda t: (buf, (p, t,)),
            lambda t: (s[0], (ALL, t,)),
            lambda t: (s[1], (t % 2, t // 2,)),
        )
    if p == 1:
        return (
            lambda t: (buf, (p, ALL, t % 2, ALL, t // 2,)),
            lambda t: (s[0], (t,)),
            lambda t: (s[1], (t,)),
        )
    return (
        lambda t: (buf, (p, ALL, ALL, t,)),
        lambda t: (s[0], (ALL, t % 2, t // 2)),
        lambda t: (s[1], (t,)),
    )


FFN_LEADS = (((2, 4, 2), (2, 2)), ((4, 4), (4,)), ((4, 2, 2), (4,)))


def pack_scatter_views(buf, s, p, lanes):
    if p == 0:
        return (
            lambda t: (buf, (ALL, ALL, t, ALL, ALL, lanes,)),
            lambda t: (s[0], (t,)),
            lambda t: (s[1], (t // 2, t % 2,)),
        )
    if p == 1:
        return (
            lambda t: (buf, (ALL, t // 2, ALL, t % 2, ALL, lanes,)),
            lambda t: (s[0], (ALL, t,)),
            lambda t: (s[1], (t,)),
        )
    return (
        lambda t: (buf, (t, ALL, ALL, ALL, ALL, lanes,)),
        lambda t: (s[0], (t // 2, ALL, t % 2,)),
        lambda t: (s[1], (t,)),
    )


PACK_LEADS = (((4, 2, 2), (2, 2)), ((4, 4), (4,)), ((2, 4, 2), (4,)))


def key_scatter_views(buf, s, p):
    rows = pl.ds(*KV_ROWS[p])
    if p == 0:
        return (
            lambda t: (buf, (ALL, ALL, t, rows, ALL,)),
            lambda t: (s[0], (ALL, t,)),
            lambda t: (s[1], (t,)),
        )
    if p == 1:
        return (
            lambda t: (buf, (t, ALL, ALL, rows, ALL,)),
            lambda t: (s[0], (ALL, t,)),
            lambda t: (s[1], (t,)),
        )
    return (
        lambda t: (buf, (ALL, t, ALL, rows, ALL,)),
        lambda t: (s[0], (t, ALL,)),
        lambda t: (s[1], (t,)),
    )


def spread(count, width, first):
    shape = (width * count, 16 * count)
    row, col = iota(shape, 0), iota(shape, 1)
    core, z, lo, r = col // 128, (col // 32) % 4, (col // 16) % 2, col % 16
    f = z * 4 + lo * 2 + core
    inside = (r >= first) & (r < first + width)
    return jnp.where(inside & (row == f * width + r - first), 1.0, 0.0).astype(BF)


def tile_rows(buf, y, hi, lanes):
    return buf[:, y, hi, :, :, :, lanes].reshape(256, lanes.stop - lanes.start)


def tile_order(i):
    return jnp.where(i >= 3, 1, 0) + jnp.where(i >= 6, 1, 0)


def key_bias(table, co, p, r, lanes):
    shape = (8, 256) if lanes else (256, 128)
    block = iota(shape, 1 if lanes else 0) // 16
    u, v = block // 4, block % 4
    c = ORDERS[p][2]
    rel = {2: (u, v, r), 0: (r, u, v), 1: (u, r, v)}[c]
    x, y, z = ((co[d] + rel[d]) % 4 for d in range(3))

    def chip(x, y, z):
        slot = (y * 2 + x // 2) * 2 + z // 2
        got = jnp.zeros(shape, jnp.int32)
        for i in range(16):
            got = got + jnp.where(slot == i, table[i], 0)
        return got * 8 + (z % 2) * 4 + (x % 2) * 2

    zero = jnp.zeros(shape, jnp.int32)
    mine = chip(zero + co[0], zero + co[1], zero + co[2])
    return jnp.where(chip(x, y, z) < mine, 0.0, MASKED)


def stage_tile(kv, kst, slot, r, i):
    rows = pl.ds(pl.multiple_of(i * 16, 16), 16)

    @pl.when(i < 3)
    def _():
        kst[slot] = kv[:, :, r, rows, :].reshape(256, 512)

    @pl.when((i >= 3) & (i < 6))
    def _():
        kst[slot] = kv[r, :, :, rows, :].reshape(256, 512)

    @pl.when(i >= 6)
    def _():
        kst[slot] = kv[:, r, :, rows, :].reshape(256, 512)


def store_tile(dkv, r, i, value):
    rows = pl.ds(pl.multiple_of(i * 16, 16), 16)
    value = value.reshape(4, 4, 16, 512)

    @pl.when(i < 3)
    def _():
        dkv[:, :, r, rows, :] = value

    @pl.when((i >= 3) & (i < 6))
    def _():
        dkv[r, :, :, rows, :] = value

    @pl.when(i >= 6)
    def _():
        dkv[:, r, :, rows, :] = value


def gelu_parts(gate):
    c = math.sqrt(2.0 / math.pi)
    square = gate * gate
    t = jnp.tanh(c * gate * (1.0 + 0.044715 * square))
    value = 0.5 * gate * (1.0 + t)
    slope = 0.5 * (1.0 + t) + 0.5 * gate * (1.0 - t * t) * (c * (1.0 + 3 * 0.044715 * square))
    return value, slope


def pair(buf, m, z):
    return jnp.concatenate([buf[m, z, 0].reshape(D, 128), buf[m, z, 1].reshape(D, 128)], axis=1)


def first_kernel(
    table, wp, gx, fp, tok, cot,
    out_o, mixg_o, kv, q, gs, dl, fg, gwo, gg_o, w, gains_o,
    wbuf, fbuf, wo, ghave, ggot, bias, kst, s_buf, o, den, osib, densib, nf, fsum, fsib, fgr, nsib,
    gate_s, up_s, hid, attended_s, ssem, rsem,
):
    co = coords()
    me = co[3]
    copies = Copies(co, ssem, rsem)
    wait_greeting = greet(co)

    x, y, z = co[:3]
    wbuf[me, y, x // 2, z, x % 2] = wp[...]
    fbuf[:, z, x % 2, y, x // 2] = fp[...]
    ghave[0] = gx[...]
    tokens = tok[...].astype(F32)
    for p in range(3):
        for r in range(4):
            bias[p * 4 + r] = key_bias(table, co, p, r, True)
    wait_greeting()

    weights = Gather(copies, weight_view(wbuf, me, (pl.ds(0, 256), pl.ds(256, 256), pl.ds(512, 384))), (0, 1, 2))
    ffn = Gather(copies, ffn_view(fbuf), (0, 1, 2))
    gains = Everywhere(copies, ghave, ggot)
    gains.send(0)
    weights.phase(0)
    ffn.phase(0)
    gains.fold(0)
    gains.send(1)
    weights.wait_all()
    weights.phase(1)
    gains.fold(1)
    gains.send(2)
    ffn.wait_all()
    ffn.phase(1)
    weights.wait_all()
    weights.phase(2)
    gains.fold(2)
    gains.send(3)
    ffn.wait_all()
    ffn.phase(2, forward=True)
    gains.fold(3)
    for i in range(4):
        gains_o[i:i + 1, :] = ghave[4, i:i + 1, :].astype(F32)
    gains_o[4:8, :] = jnp.zeros((4, D), F32)
    gain_in, gain_att, gain_ffn, gain_out = (gains_o[i:i + 1, :] for i in range(4))
    normed_in = norm_forward(tokens, gain_in).astype(BF)

    weights.wait(0)
    weights.wait(1)
    swap_in = copies.sibling(wbuf.at[me, :, :, :, :, :, pl.ds(0, 512)], wbuf.at[me, :, :, :, :, :, pl.ds(0, 512)])
    weights.wait(2)
    swap_out = copies.sibling(wbuf.at[me, :, :, :, :, :, pl.ds(512, 384)], wbuf.at[me, :, :, :, :, :, pl.ds(512, 384)])
    picks = [spread(16, 5, 5 * k) for k in range(3)]
    swap_in.wait_recv()
    for c in range(8):
        rows = tile_rows(wbuf, c // 2, c % 2, slice(0, 512))
        for k in range(3):
            w[80 * c:80 * c + 80, 512 * k:512 * k + 512] = nn(picks[k], rows).astype(BF)

    kv[0, 0, 0] = nn(normed_in, w[:, 1024:1536]).astype(BF)
    keys = KeyGather(copies, kv)
    keys.start()
    for h in range(H):
        q[h, me] = nn(normed_in, w[:, 256 * h:256 * h + 256]).astype(BF)
    q_copy = copies.sibling(q.at[:, me], q.at[:, me])
    ffn.forward(ffn_halves)
    keys.mid()

    swap_out.wait_recv()
    pick_lo, pick_hi = spread(16, 8, 0), spread(16, 8, 8)
    for c in range(8):
        rows = tile_rows(wbuf, c // 2, c % 2, slice(512, 896))
        wo[128 * c:128 * c + 128, 0:384] = nn(pick_lo, rows).astype(BF)
        wo[128 * c:128 * c + 128, 384:640] = nn(pick_hi, rows[:, 0:256]).astype(BF)
    keys.last()

    q_copy.wait_recv()
    key, value = kv[0, 0, 0, :, 0:256], kv[0, 0, 0, :, 256:512]
    s = nt(q[...].reshape(1024, HD), key)
    seen = iota((1024, 128), 1) + me * 128 <= iota((1024, 128), 0) % 256
    e = jnp.where(seen, jnp.exp2(jnp.tanh(s * SCORE) * EXPO), 0.0)
    den[...] = e.reshape(H, 2, 128, 128)
    o[...] = nn(e.astype(BF), value).reshape(H, 2, 128, HD)

    def attend(first, count):
        def scores(t, slot):
            stage = t // 8
            r = stage + (stage // 2) * (1 - 2 * (stage % 2))
            stage_tile(kv, kst, slot, r, t % 8)
            s_buf[slot] = nt(q[...].reshape(1024, HD), kst[slot, :, 0:256])

        def finish(t, slot):
            stage = t // 8
            r = stage + (stage // 2) * (1 - 2 * (stage % 2))
            low = bias[tile_order(t % 8) * 4 + r, 0:1, :]
            e = jnp.exp2(jnp.tanh(s_buf[slot] * SCORE) * EXPO + low)
            den[...] += (e[:, :128] + e[:, 128:]).reshape(H, 2, 128, 128)
            o[...] += nn(e.astype(BF), kst[slot, :, 256:512]).reshape(H, 2, 128, HD)

        last = first + count - 1
        scores(first, 0)

        def body(u, carry):
            t = first + 2 * u
            scores(t + 1, 1)
            finish(t, 0)
            scores(jnp.minimum(t + 2, last), 0)
            finish(t + 1, 1)
            return carry

        lax.fori_loop(0, count // 2, body, 0)

    attend(0, 8)
    keys.forward()
    keys.wait_edges()
    attend(8, 16)
    keys.wait_opposite()
    attend(24, 8)

    o_copy = copies.sibling(o.at[:, 1 - me], osib)
    den_copy = copies.sibling(den.at[:, 1 - me], densib)
    o_copy.wait_recv()
    den_copy.wait_recv()
    for h in range(H):
        total = jnp.sum(den[h, me] + densib[h], axis=-1, keepdims=True)
        attended_s[:, HD * h:HD * h + HD] = (o[h, me] + osib[h]) / total
    attended = attended_s[...]
    attended_low = attended.astype(BF)
    attention_out = nn(attended_low, wo[...])
    mixed = tokens + norm_forward(attention_out, gain_att)
    nf[me] = norm_forward(mixed, gain_ffn).astype(BF)
    nf_copy = copies.sibling(nf.at[me], nf.at[me])
    ffn.wait_all()
    nf_copy.wait_recv()

    fsum[...] = jnp.zeros_like(fsum)

    def ffn_forward(i, carry):
        rows = nf[...].reshape(256, D)
        gate = nn(rows, pair(fbuf, 0, i))
        up = nn(rows, pair(fbuf, 1, i))
        gate_s[i] = gate
        up_s[i] = up
        low = (gelu_parts(gate)[0] * up).astype(BF)
        hid[i] = low
        fsum[...] += nt(low, pair(fbuf, 2, i)).reshape(2, ROWS, D)
        return carry

    lax.fori_loop(0, 4, ffn_forward, 0)
    f_copy = copies.sibling(fsum.at[1 - me], fsib)
    f_copy.wait_recv()
    ffn_out = fsum[me] + fsib[...]
    out_o[...] = (mixed + norm_forward(ffn_out, gain_out)).astype(BF)
    cotangent = cot[...].astype(F32)
    ffn_out_grad, part_out = norm_backward(ffn_out, gain_out, cotangent)
    fgr[me] = ffn_out_grad.astype(BF)
    fgr_copy = copies.sibling(fgr.at[me], fgr.at[me])
    fgr_copy.wait_recv()
    copies.sent(f_copy)
    fsum[...] = jnp.zeros_like(fsum)

    def ffn_backward(i, carry):
        rows = nf[...].reshape(256, D)
        grads = fgr[...].reshape(256, D)
        gates, ups, downs = pair(fbuf, 0, i), pair(fbuf, 1, i), pair(fbuf, 2, i)
        hidden_grad = nn(grads, downs)
        value, slope = gelu_parts(gate_s[i])
        gate_low = (hidden_grad * up_s[i] * slope).astype(BF)
        up_low = (hidden_grad * value).astype(BF)
        for m, got in enumerate((tn(rows, gate_low), tn(rows, up_low), tn(grads, hid[i]))):
            got = got.astype(BF)
            fg[m, i, 0] = got[:, 0:128].reshape(4, 2, 80, 128)
            fg[m, i, 1] = got[:, 128:256].reshape(4, 2, 80, 128)
        fsum[...] += (nt(gate_low, gates) + nt(up_low, ups)).reshape(2, ROWS, D)
        return carry

    lax.fori_loop(0, 4, ffn_backward, 0)
    n_copy = copies.sibling(fsum.at[1 - me], nsib)
    n_copy.wait_recv()
    normed_ffn_grad = fsum[me] + nsib[...]
    mixed_part, part_ffn = norm_backward(mixed, gain_ffn, normed_ffn_grad)
    mixed_grad = cotangent + mixed_part
    mixg_o[...] = mixed_grad
    out_grad, part_att = norm_backward(attention_out, gain_att, mixed_grad)
    out_grad_low = out_grad.astype(BF)
    zero = jnp.zeros((1, D), F32)
    gg_o[...] = jnp.concatenate([zero, part_att, part_ffn, part_out, zero, zero, zero, zero], axis=0)

    grad = nt(out_grad_low, wo[...]).astype(BF)
    for h in range(H):
        cols = slice(HD * h, HD * h + HD)
        lane_sum = den[h, me] + densib[h]
        total = jnp.sum(lane_sum, axis=-1, keepdims=True)
        part = grad[:, cols].astype(F32)
        gs[h, me] = (part / total).astype(BF)
        delta = nt_exact(jnp.ones((8, HD), F32), part * attended[:, cols])
        dl[h, me] = delta / nt_exact(jnp.ones((8, 128), F32), lane_sum)
    g_copy = copies.sibling(gs.at[:, me], gs.at[:, me])
    dl_copy = copies.sibling(dl.at[:, me], dl.at[:, me])
    output_part = tn(attended_low, out_grad_low).astype(BF)
    for c in range(8):
        rows = output_part[128 * c:128 * c + 128, :]
        lo = tn(pick_lo, rows[:, 0:384])
        hi = tn(pick_hi, rows[:, 384:640])
        got = jnp.concatenate([lo[:, 0:256] + hi, lo[:, 256:384]], axis=1).astype(BF)
        gwo[:, c // 2, c % 2] = got.reshape(2, 4, 2, 16, 384)
    g_copy.wait_recv()
    dl_copy.wait_recv()
    copies.drain()


def second_kernel(
    table, tok, kv, q, gs, dl, fg, gwo, gg, w, gains, mixg,
    tgrad_o, qkv_o, wo_o, ffn_o, gain_o,
    dkv, bias, kst, s_buf, p_buf, dq, dqsib, dkown, dqkv, gqkv, gqsib, gosib, gosum, ghave, ggot, *rest,
):
    rs, (ssem, rsem) = rest[:-2], rest[-2:]
    co = coords()
    me = co[3]
    copies = Copies(co, ssem, rsem)
    wait_greeting = greet(co)
    rel = lambda d, s: s
    ab = absolute(co)

    def group(n):
        return rs[5 * n:5 * n + 3], rs[5 * n + 3:5 * n + 5]

    for p in range(3):
        for r in range(4):
            bias[p * 4 + r] = key_bias(table, co, p, r, False)
    wait_greeting()
    swap = copies.sibling(gwo.at[1 - me], gosib)
    ffns = []
    for p in range(3):
        r, s = group(p)
        ffns.append(Scatter(copies, p, ffn_scatter_views(fg, s, p), ab, r, s))
    keys = []
    for p in range(3):
        r, s = group(3 + p)
        keys.append(Scatter(copies, p, key_scatter_views(dkv, s, p), rel, r, s))
    outs = []
    for p in range(3):
        r, s = group(6 + p)
        outs.append(Scatter(copies, p, pack_scatter_views(gosum, s, p, pl.ds(128 * p, 128)), ab, r, s))
    for f in ffns:
        f.send(0)
    swap.wait_recv()
    for yy in range(4):
        for hi in range(2):
            gosum[yy, hi] = (gwo[me, yy, hi].astype(F32) + gosib[yy, hi].astype(F32)).astype(BF)
    for f in outs:
        f.send(0)

    delta = jnp.concatenate([dl[h, c][0:1, :] for h in range(H) for c in range(2)], axis=1)

    key, value = kv[0, 0, 0, :, 0:256], kv[0, 0, 0, :, 256:512]
    rows, grads = q[...].reshape(1024, HD), gs[...].reshape(1024, HD)
    tan = jnp.tanh(nt(key, rows) * SCORE)
    seen = iota((128, 1024), 0) + me * 128 <= iota((128, 1024), 1) % 256
    e = jnp.where(seen, jnp.exp2(tan * EXPO), 0.0)
    ds = (e * (nt(value, grads) - delta) * (1.0 - tan * tan)).astype(BF)
    dkown[:, 0:256] = nn(ds, rows) * (1.0 / 16)
    dkown[:, 256:512] = nn(e.astype(BF), grads)
    dq[...] = tn(ds, key).reshape(H, 2, 128, HD)

    def attend(r):
        def scores(t, slot):
            stage_tile(kv, kst, slot, r, t)
            s_buf[slot] = nt(kst[slot, :, 0:256], q[...].reshape(1024, HD))
            p_buf[slot] = nt(kst[slot, :, 256:512], gs[...].reshape(1024, HD))

        def finish(t, slot):
            low = jnp.concatenate([bias[tile_order(t) * 4 + r]] * 8, axis=1)
            tan = jnp.tanh(s_buf[slot] * SCORE)
            e = jnp.exp2(tan * EXPO + low)
            ds = ((e * (p_buf[slot] - delta)) * (1.0 - tan * tan)).astype(BF)
            dv = nn(e.astype(BF), gs[...].reshape(1024, HD)).astype(BF)
            dk = (nn(ds, q[...].reshape(1024, HD)) * (1.0 / 16)).astype(BF)
            dq[...] += tn(ds, kst[slot, :, 0:256]).reshape(H, 2, 128, HD)
            store_tile(dkv, r, t, jnp.concatenate([dk, dv], axis=1))

        scores(0, 0)

        def body(u, carry):
            t = 2 * u
            scores(t + 1, 1)
            finish(t, 0)
            scores(jnp.minimum(t + 2, 7), 0)
            finish(t + 1, 1)
            return carry

        lax.fori_loop(0, 4, body, 0)

    attend(2)
    for f in keys:
        f.send(0, (2,))
    for f in ffns + outs:
        f.fold(0)
        f.send(1)
    attend(1)
    for f in keys:
        f.send(0, (1,))
    for f in ffns + outs:
        f.fold(1)
        f.send(2)
    attend(3)
    for f in keys:
        f.send(0, (3,))
    for p, f in enumerate(ffns):
        def write(at, got, p=p):
            ffn_o[p] = got
        f.total(2, write)
    for p, f in enumerate(outs):
        def write(at, got, p=p):
            wo_o[:, 128 * p:128 * p + 128] = got
        f.total(2, write)
    attend(0)

    q_copy = copies.sibling(dq.at[:, 1 - me], dqsib)
    tokens = tok[...].astype(F32)
    gain_in = gains[0:1, :]
    normed_in = norm_forward(tokens, gain_in).astype(BF)
    q_copy.wait_recv()
    for h in range(H):
        dqkv[:, HD * h:HD * h + HD] = ((dq[h, me] + dqsib[h]) * (1.0 / 16)).astype(BF)
    for f in keys:
        f.fold(0)
        f.send(1)
    query_part = tn(normed_in, dqkv[:, 0:1024]).astype(BF)
    for f in keys:
        f.fold(1)
        f.send(2)
    for p, f in enumerate(keys):
        first, size = KV_ROWS[p]

        def write(at, got, first=first, size=size):
            got = got + dkown[first:first + size, :]
            dqkv[first:first + size, 1024:1536] = got.astype(BF)

        f.total(2, write)
    key_part = tn(normed_in, dqkv[:, 1024:1536]).astype(BF)

    picks = [spread(16, 5, 5 * k) for k in range(3)]
    for c in range(8):
        rows = slice(80 * c, 80 * c + 80)
        got = tn(picks[0], query_part[rows, 0:512]) + tn(picks[1], query_part[rows, 512:1024])
        got = got + tn(picks[2], key_part[rows, :])
        gqkv[:, c // 2, c % 2] = got.astype(BF).reshape(2, 4, 2, 16, 512)
    swap = copies.sibling(gqkv.at[1 - me], gqsib)
    normed_in_grad = nt(dqkv[...], w[...])
    input_part, part_in = norm_backward(tokens, gain_in, normed_in_grad)
    tgrad_o[...] = (mixg[...] + input_part).astype(BF)
    ghave[0] = jnp.concatenate([part_in, gg[1:8, :]], axis=0)
    sums = Everywhere(copies, ghave, ggot)
    sums.send(0)
    swap.wait_recv()
    sums.fold(0)
    sums.send(1)
    for yy in range(4):
        for hi in range(2):
            gqsib[yy, hi] = (gqkv[me, yy, hi].astype(F32) + gqsib[yy, hi].astype(F32)).astype(BF)
    lanes = ((0, 128), (128, 128), (256, 256))
    qkvs = []
    for p in range(3):
        r, s = group(9 + p)
        view = pack_scatter_views(gqsib, s, p, pl.ds(*lanes[p]))
        qkvs.append(Scatter(copies, p, view, ab, r, s))
    for f in qkvs:
        f.send(0)
    sums.fold(1)
    sums.send(2)
    for f in qkvs:
        f.fold(0)
        f.send(1)
    sums.fold(2)
    sums.send(3)
    for f in qkvs:
        f.fold(1)
        f.send(2)
    sums.fold(3)
    index = lax.axis_index("ctx") * 16 + lax.axis_index("fsdp")
    shape = (D, 128)
    mine = (iota(shape, 0) == index * 5 + iota(shape, 1)) & (iota(shape, 1) < 5)
    gain_o[...] = nn_exact(ghave[4], jnp.where(mine, 1.0, 0.0))
    for p, f in enumerate(qkvs):
        def write(at, got, p=p):
            qkv_o[:, lanes[p][0]:lanes[p][0] + lanes[p][1]] = got
        f.total(2, write)
    copies.drain()


def sds(shape, dtype):
    return jax.ShapeDtypeStruct(shape, dtype)


VM = pl.BlockSpec(memory_space=pltpu.VMEM)
SM = pl.BlockSpec(memory_space=pltpu.SMEM)
FFN_SHAPE = (3, 4, 2, 4, 2, 80, 128)
KV_SHAPE = (4, 4, 4, ROWS, 512)


def first_call(table, wp, gx, fp, tok, cot):
    outs = [
        sds((ROWS, D), BF), sds((ROWS, D), F32), sds(KV_SHAPE, BF), sds((H, 2, ROWS, HD), BF),
        sds((H, 2, ROWS, HD), BF), sds((H, 2, 8, ROWS), F32), sds(FFN_SHAPE, BF),
        sds((2, 4, 2, 4, 2, 16, 384), BF), sds((8, D), F32), sds((D, 1536), BF), sds((8, D), F32),
    ]
    vm = pltpu.VMEM
    scratch = [
        vm((2, 4, 2, 4, 2, 16, 896), BF), vm(FFN_SHAPE, BF), vm((H * HD, D), BF),
        vm((5, 16, D), BF), vm((4, 3, 16, D), BF), vm((12, 8, 256), F32), vm((2, 256, 512), BF),
        vm((2, 1024, 256), F32), vm((H, 2, ROWS, HD), F32), vm((H, 2, ROWS, 128), F32),
        vm((H, ROWS, HD), F32), vm((H, ROWS, 128), F32), vm((2, ROWS, D), BF), vm((2, ROWS, D), F32),
        vm((ROWS, D), F32), vm((2, ROWS, D), BF), vm((ROWS, D), F32), vm((4, 256, 256), F32),
        vm((4, 256, 256), F32), vm((4, 256, 256), BF), vm((ROWS, H * HD), F32),
        pltpu.SemaphoreType.DMA((160,)), pltpu.SemaphoreType.DMA((160,)),
    ]
    return pl.pallas_call(
        first_kernel,
        out_shape=outs,
        in_specs=[SM] + [VM] * 5,
        out_specs=[VM] * len(outs),
        scratch_shapes=scratch,
        compiler_params=pltpu.CompilerParams(
            collective_id=0, has_side_effects=True, vmem_limit_bytes=VMEM_LIMIT
        ),
    )(table, wp, gx, fp, tok, cot)


def scatter_scratch(leads, block, dtype=BF):
    first, second = leads
    vm = pltpu.VMEM
    return [
        vm((3,) + first + block, dtype), vm((3,) + second + block, dtype), vm((3,) + block, dtype),
        vm(first + block, dtype), vm(second + block, dtype),
    ]


def second_call(*args):
    outs = [
        sds((ROWS, D), BF), sds((16, 512), F32), sds((16, 384), F32), sds((3, 80, 128), F32), sds((8, 128), F32),
    ]
    vm = pltpu.VMEM
    scratch = [
        vm(KV_SHAPE, BF), vm((12, 256, 128), F32), vm((2, 256, 512), BF), vm((2, 256, 1024), F32),
        vm((2, 256, 1024), F32), vm((H, 2, ROWS, HD), F32), vm((H, ROWS, HD), F32), vm((ROWS, 512), F32),
        vm((ROWS, 1536), BF), vm((2, 4, 2, 4, 2, 16, 512), BF), vm((4, 2, 4, 2, 16, 512), BF),
        vm((4, 2, 4, 2, 16, 384), BF), vm((4, 2, 4, 2, 16, 384), BF), vm((5, 8, D), F32), vm((4, 3, 8, D), F32),
    ]
    for p in range(3):
        scratch += scatter_scratch(FFN_LEADS[p], (80, 128))
    for p in range(3):
        scratch += scatter_scratch(((4, 4), (4,)), (KV_ROWS[p][1], 512))
    for p in range(3):
        scratch += scatter_scratch(PACK_LEADS[p], (16, 128))
    for p in range(3):
        scratch += scatter_scratch(PACK_LEADS[p], (16, (128, 128, 256)[p]))
    scratch += [pltpu.SemaphoreType.DMA((160,)), pltpu.SemaphoreType.DMA((160,))]
    return pl.pallas_call(
        second_kernel,
        out_shape=outs,
        in_specs=[SM] + [VM] * (len(args) - 1),
        out_specs=[VM] * len(outs),
        scratch_shapes=scratch,
        compiler_params=pltpu.CompilerParams(
            collective_id=1, has_side_effects=True, vmem_limit_bytes=VMEM_LIMIT
        ),
    )(*args)


def shards(
    tokens, query_weight, key_weight, value_weight, output_weight, gate_weight, up_weight, down_weight,
    input_gain, attention_gain, feedforward_gain, output_gain, block_table, cotangent,
):
    index = lax.axis_index("ctx") * 16 + lax.axis_index("fsdp")
    left = jnp.concatenate(
        [query_weight[:, 0:512], query_weight[:, 512:1024], jnp.concatenate([key_weight, value_weight], axis=1),
         jnp.zeros((1, 512), BF)], axis=0)
    right = jnp.concatenate(
        [output_weight[:, 0:384], jnp.pad(output_weight[:, 384:640], ((0, 0), (0, 128)))], axis=0)
    wp = jnp.concatenate([left, right], axis=1)
    gains = jnp.stack([input_gain, attention_gain, feedforward_gain, output_gain])
    gx = jnp.where(jnp.arange(D) // 5 == index, jnp.tile(gains, (1, 128)), 0).astype(BF)
    gx = jnp.pad(gx, ((0, 12), (0, 0)))
    fp = jnp.stack([gate_weight, up_weight, down_weight.T])
    output, mixed_grad, kv, q, gs, dl, fg, gwo, gg, w, gains = first_call(
        block_table, wp, gx, fp, tokens, cotangent)
    tokens_gradient, qkv, out, ffn, gain = second_call(
        block_table, tokens, kv, q, gs, dl, fg, gwo, gg, w, gains, mixed_grad)
    return (
        output,
        tokens_gradient,
        jnp.concatenate([qkv[0:5], qkv[5:10]], axis=1),
        qkv[10:15, 0:256],
        qkv[10:15, 256:512],
        jnp.concatenate([out[0:8], out[8:16, 0:256]], axis=1),
        ffn[0],
        ffn[1],
        ffn[2].T,
        gain[0, 0:5],
        gain[1, 0:5],
        gain[2, 0:5],
        gain[3, 0:5],
    )


def solution(mesh):
    both = P(("ctx", "fsdp"))
    rows = P(("ctx", "fsdp"), None)
    return jax.shard_map(
        shards,
        mesh=mesh,
        in_specs=(
            rows, rows, rows, rows, rows, P("ctx", "fsdp"), P("ctx", "fsdp"), P("fsdp", "ctx"),
            both, both, both, both, P(), rows,
        ),
        out_specs=(
            rows, rows, rows, rows, rows, rows, P("ctx", "fsdp"), P("ctx", "fsdp"), P("fsdp", "ctx"),
            both, both, both, both,
        ),
        check_vma=False,
    )
```

time: 2540 us -> 246 us (0.10)
  blocking collectives: 1170 us -> 0 us
  waiting for transfers between devices: 1090 us -> 0 us
  Pallas kernels: 0 us -> 228 us
  matrix products: 150 us -> 0 us
  local copies, waits for them, and re-layouts: 69.9 us -> 11.6 us
    all_gather x14 -> x0, blocking collectives: 1030 us -> none  [the longest x2 348 us: fetch_attention(): lax.all_gather(value_weight, ('ctx', 'fsdp'), axis=0, tiled=True)]
    reduce_scatter x8 -> x0, waiting for transfers between devices: 515 us -> none  [the longest x1 97.2 us: shards(): lax.psum_scatter(join_query(query_parts), 'fsdp', scatter_dimension=0, ti...]
    all_gather x8 -> x0, waiting for transfers between devices: 474 us -> none  [the longest x2 348 us: fetch_attention(): lax.all_gather(output_weight, ('ctx', 'fsdp'), axis=0, tiled=True)]
    pallas_call x0 -> x2, Pallas kernels: none -> 228 us  [the longest x1 120 us: second_call(): pl.pallas_call(second_kernel, out_shape=outs, in_specs=[SM] + [VM] * (len...]
    dot_general x49 -> x0, matrix products: 150 us -> none  [the longest x19 59.6 us: outer_cols(): lax.dot_general(left, right, (((1,), (1,)), ((), ())), preferred_element_...]
    unnamed x2 -> x0, blocking collectives: 133 us -> none
    all_to_all x2 -> x0, waiting for transfers between devices: 95 us -> none  [the longest x1 95 us: shards(): lax.all_to_all(join_query(summed).reshape(fsdp_size, own_rows, H * HD), '...]
  transfers between devices with their start and end apart: 19 -> 0, of which waited for: 11 -> 0; matrix products, arithmetic and copies ran while one was open for 3% -> 0% of each run, Pallas kernels for 0% -> 0%
where the time goes in v1:
time: 246 us; the launch traced here: 245 us
  Pallas kernels  228 us (93%)
  local copies, waits for them, and re-layouts  11.6 us (5%)
  other arithmetic  4.7 us (2%)
    pallas_call x1, Pallas kernels, second_call(): pl.pallas_call(second_kernel, out_shape=outs, in_specs=[SM] + [VM] * (len...  120 us
    pallas_call x1, Pallas kernels, first_call(): pl.pallas_call(first_kernel, out_shape=outs, in_specs=[SM] + [VM] * 5, ou...  108 us

profile of v1, /device:TPU:0, one launch (start us, length us, event | category | flops | bytes accessed | tf_op | source)
XLA Modules:
  0.0 245.1 jit_solution(13236556355757489407)
XLA Ops:
  0.7 0.7 pad_maximum_fusion.3
  1.4 0.7 slice.54
  2.1 0.7 slice.53
  2.8 0.7 fusion.11
  3.5 1.3 fusion.4.wp
  4.8 1.4 pad_maximum_fusion.fp
  6.2 0.2 tile.10
  6.5 0.6 pad.9.gx
  7.1 108.2 %shard_map.237 = (bf16[128,640]{1,0:T(8,128)(2,1)}, f32[128,640]{1,0:T(8,128)}, bf16[4,4,4,128,512]{4,3,2,1,0:T(8,128)(2,1)}, bf16[4,2,128,256]{3,2,1,0:T(8,128)...) custom-call(s32[16]{0:T(128)} %table.3, ...), custom_call_target="tpu_custom_call" | custom-call | tf_op jit(solution)/shard_map/pallas_call | solution.py:891
  115.3 0.0 copy-start
  115.3 120.0 %shard_map.238 = (bf16[128,640]{1,0:T(8,128)(2,1)}, f32[16,512]{1,0:T(8,128)}, f32[16,384]{1,0:T(8,128)}, f32[3,80,128]{2,1,0:T(8,128)}, f32[8,128]{1,0:T(8,128)}) custom-call(s32[16]{0:T(128)} %table.3, bf16[128,640]{1,0:T(8,128)(2,1)} %tok.3, bf16[4,4,4,128,512]{4,3,2,1,0:T(8,128)(2,1)} %get-tuple-element.30.kv, ...), custom_call_target="tpu_custom_call" | custom-call | tf_op jit(solution)/shard_map/pallas_call | solution.py:932
  235.3 1.4 slice_bitcast_fusion.3
  236.6 0.7 slice.60
  237.3 0.7 slice.59
  238.0 0.6 pad_maximum_fusion.2
  238.6 1.3 fusion.9
  240.0 0.8 fusion.10
  240.8 0.6 pad_maximum_fusion.1
  241.4 1.5 slice_bitcast_fusion
  242.9 0.0 copy-done
  242.9 0.7 copy.29
  243.5 1.6 copy.30
  (4 shorter events, 0.0 us)
Async XLA Ops:
  115.3 127.6 %copy-start = (bf16[128,640]{1,0:T(8,128)(2,1)S(1)}, bf16[128,640]{1,0:T(8,128)(2,1)}, u32[]{:S(2)}) copy-start(bf16[128,640]{1,0:T(8,128)(2,1)} %get-tuple-element.71) | copy-start | bytes 491524
